TPU v7x, 32 devices: a whole 2x2x4 slice. The times are simulated.
32 devices in a mesh: freq: 2 (over x), row: 16 (over z, y, core).
Axes of the slice: x: 2, y: 2, z: 4, core: 2. Of those that a mesh axis runs over, the one named last changes fastest.
Arguments:
- p_panel: float32 [2, 256, 256], P(None, ('freq', 'row')), parts along dimension 1, may hold values from -0.375 to 0.375
- eps_coef: float32 [4, 201, 201], P('freq'), parts along dimension 0, may hold values from -3 to 3
- inv_coef: float32 [4, 201, 201], P('freq'), parts along dimension 0, may hold values from -3 to 3
- wave: float32 [8], P('freq'), parts along dimension 0, may hold values from 0.02 to 0.06
- harmonics: int32 [2, 2048], replicated, may hold values from -50 to 50, as said below
- panel: int32 [256], replicated, may hold values from 0 to 4095, as said below
- row_target: int32 [128], replicated, may hold values from 0 to 127, as said below
Outputs:
- omega: float32 [2, 256, 4096], P(None, ('freq', 'row')), parts along dimension 1
There are 2 independent parts, one for each index of `freq`. A program takes and returns all parts, laid end to end along the dimension named above; an argument that names none is the same for every part. Nothing has to cross between parts.
Inputs may be any that keep to these rules, and one draw needn't show every extreme that they name: `harmonics`: all pairs (m, n) are distinct. `panel`: 256 distinct row indices of Q. row_target[s] = 8 rho(s mod 16) + tau(s // 16) for a permutation rho of 0 .. 15 and a permutation tau of 0 .. 7, both drawn from the seed; each window row appears once.
All inputs are finite; a program needn't handle non-finite values.
Results may differ from a plain program's by a relative error of at most 0.0003.
Values sent between devices are 32-bit elements; how exact they have to be, the bound alone decides.
A program may use at most 128 MiB of HBM per device.

v0:
```python
import jax
import jax.numpy as jnp
from jax import lax
from jax.sharding import PartitionSpec as P

HARM_DEV = 128


def stack_tables(eps_coef, inv_coef):
    flat_eps = eps_coef.reshape(2, -1)
    flat_inv = inv_coef.reshape(2, -1)
    return jnp.transpose(jnp.concatenate([flat_eps, flat_inv], 1), (1, 0))


def build_panel(harmonics, panel, coef_table, extent, wave, first_col, col_count):
    harm_total = harmonics.shape[1]
    row_block = panel // harm_total
    row_harm = panel % harm_total
    m_row = jnp.take(harmonics[0], row_harm)
    n_row = jnp.take(harmonics[1], row_harm)
    col_harm = first_col + jnp.arange(col_count, dtype=jnp.int32)
    m_col = lax.dynamic_slice_in_dim(harmonics[0], first_col, col_count)
    n_col = lax.dynamic_slice_in_dim(harmonics[1], first_col, col_count)
    centre = (extent - 1) // 2
    top_rows = row_block == 0
    shift_rows = jnp.where(top_rows, extent * extent, 0).astype(jnp.int32)
    offset_m = m_row[:, None] - m_col[None, :] + centre
    offset_n = n_row[:, None] - n_col[None, :] + centre
    table_index = offset_m * extent + offset_n + shift_rows[:, None]
    looked = jnp.take(coef_table, table_index, axis=0)
    value_real = looked[:, :, 0]
    value_imag = looked[:, :, 1]
    wave_x = (wave[0] + m_row.astype(jnp.float32) * wave[2])[:, None]
    wave_y = (wave[1] + n_row.astype(jnp.float32) * wave[3])[:, None]
    on_diag = (row_harm[:, None] == col_harm[None, :]).astype(jnp.float32)
    top_half = top_rows[:, None]
    zeros_like = jnp.zeros_like(value_real)
    first_real = jnp.where(
        top_half, wave_x * wave_y * on_diag, wave_y * wave_y * on_diag - value_real
    )
    first_imag = jnp.where(top_half, zeros_like, -value_imag)
    second_real = jnp.where(
        top_half, value_real - wave_x * wave_x * on_diag, -wave_x * wave_y * on_diag
    )
    second_imag = jnp.where(top_half, value_imag, zeros_like)
    return jnp.stack(
        [
            jnp.concatenate([first_real, second_real], 1),
            jnp.concatenate([first_imag, second_imag], 1),
        ]
    )


def matmul(first_mat, second_mat):
    return jnp.dot(
        first_mat, second_mat, precision=lax.Precision.HIGHEST, preferred_element_type=jnp.float32
    )


def join_parts(right_mat):
    return jnp.concatenate([right_mat[0], right_mat[1]], 1)


def joined_product(left_mat, joined, columns):
    rows_here = left_mat.shape[1]
    stacked = left_mat.reshape(2 * rows_here, left_mat.shape[2])
    result = matmul(stacked, joined)
    real_part = result[:rows_here, :columns] - result[rows_here:, columns:]
    imag_part = result[:rows_here, columns:] + result[rows_here:, :columns]
    return jnp.stack([real_part, imag_part])


def on_device(p_panel, eps_coef, inv_coef, wave, harmonics, panel, row_target):
    extent = eps_coef.shape[1]
    coef_table = stack_tables(eps_coef, inv_coef)
    position = lax.axis_index("row")
    q_local = build_panel(harmonics, panel, coef_table, extent, wave, position * HARM_DEV, HARM_DEV)
    q_joined = join_parts(q_local)
    product_tile = joined_product(
        lax.all_gather(p_panel, "row", axis=1, tiled=True), q_joined, 2 * HARM_DEV
    )
    product_tile = jnp.take(product_tile, row_target, axis=1)
    return lax.all_to_all(product_tile, "row", split_axis=1, concat_axis=2, tiled=True)


def solution(mesh):
    in_specs = (
        P(None, ("freq", "row"), None),
        P("freq", None, None),
        P("freq", None, None),
        P("freq"),
        P(),
        P(),
        P(),
    )
    out_specs = P(None, ("freq", "row"), None)
    return jax.shard_map(
        on_device, mesh=mesh, in_specs=in_specs, out_specs=out_specs, check_vma=False
    )
```

profile of v0, /device:TPU:1, one launch (start us, length us, event | category | flops | bytes accessed | tf_op | source)
XLA Modules:
  0.0 206.8 jit_solution(3331236157330673411)
XLA Ops:
  0.0 0.7 compare_select_fusion.6
  0.7 0.8 fusion.22
  1.5 1.7 gather_fusion.2
  3.2 1.7 gather_fusion.3
  5.0 1.5 fusion.23
  6.4 2.6 %fusion.19 = (f32[256]{0:T(256)S(1)}, s32[256]{0:T(256)S(1)}, s32[256]{0:T(256)S(1)}) fusion(f32[]{:T(128)} %bitcast.2, f32[]{:T(128)} %bitcast, f32[]{:T(128)} %bitcast.5, f32[]{:T(128)} %bitcast.3, s32[256]{0:T(256)S(1)} %gather_fusion.2, s32[256]{0:T(256)S(1)} %get-tuple-element.10, s32[256]{0:T(256)S(1)} %gather_fusion.3), kind=kLoop, calls=%fused_computation.62 | loop fusion | flops 3840 | bytes 6160 | tf_op jit(solution)/shard_map/mul | solution.py:39
  9.4 2.6 %fusion.20 = (f32[256]{0:T(256)S(1)}, f32[256]{0:T(256)S(1)}, f32[256]{0:T(256)S(1)}) fusion(f32[]{:T(128)} %bitcast.5, s32[256]{0:T(256)S(1)} %get-tuple-element.8, f32[]{:T(128)} %bitcast.3, f32[]{:T(128)} %bitcast.2, s32[256]{0:T(256)S(1)} %get-tuple-element.7, f32[]{:T(128)} %bitcast), kind=kLoop, calls=%fused_computation.63 | loop fusion | flops 2560 | bytes 5136 | tf_op jit(solution)/shard_map/mul | solution.py:39
  12.0 0.7 compare_select_fusion.7
  12.7 0.7 compare_and_fusion.2
  13.3 1.0 copy.19
  14.4 0.6 reshape.230
  14.9 1.0 copy.20
  16.0 0.6 reshape.231
  16.6 0.5 pad_maximum_fusion
  17.0 19.3 %copy.21 = f32[2,80802]{0,1:T(8,128)} copy(f32[2,80802]{1,0:T(2,128)S(1)} %pad_maximum_fusion) | data formatting | bytes 1292832 | tf_op jit(solution)/shard_map/concatenate | solution.py:12
  36.3 121.6 %gather_fusion = f32[32768,2]{1,0:T(8,128)} fusion(f32[80802,2]{1,0:T(8,128)} %bitcast.43, s32[32768]{0:T(1024)S(1)} %fusion.12), kind=kCustom, calls=%fused_computation.2 | custom fusion | bytes 655360 | tf_op jit(solution)/shard_map/jit(_take)/gather | solution.py:30
  157.9 9.7 %copy.22 = f32[256,128,2]{1,0,2:T(8,128)S(1)} copy(f32[256,128,2]{2,1,0:T(8,128)} %bitcast.46) | data formatting | bytes 524288 | tf_op jit(solution)/shard_map/jit(_take)/gather | solution.py:30
  167.6 23.7 %all_gather.3 = f32[2,128,256]{2,1,0:T(8,128)S(1)} all-gather(f32[2,8,256]{2,1,0:T(8,128)S(1)} %copy-done), channel_id=1, replica_groups=mesh['freq'=2,'row'=16] {'row'}, dimensions={1}, use_global_device_ids=true | all-gather | bytes 278528 | tf_op jit(solution)/shard_map/all_gather | solution.py:80
  191.4 0.3 fusion.7
  191.6 1.0 convolution_bitcast_fusion
  192.9 0.9 gather_fusion.1
  193.8 0.2 select_bitcast_fusion
  194.0 12.1 %all_to_all.18 = f32[2,128,256]{2,0,1:T(2,128)S(1)} all-to-all(f32[2,128,256]{2,0,1:T(2,128)S(1)} %select_bitcast_fusion), channel_id=1, replica_groups=mesh['freq'=2,'row'=16] {'row'}, dimensions={1} | all-to-all | bytes 524288 | tf_op jit(solution)/shard_map/all_to_all | solution.py:83
  206.1 0.7 copy.24
  (12 shorter events, 0.6 us)
Async XLA Ops:
  157.9 9.7 %copy-start = (f32[2,8,256]{2,1,0:T(8,128)S(1)}, f32[2,8,256]{2,1,0:T(8,128)}, u32[]{:S(2)}) copy-start(f32[2,8,256]{2,1,0:T(8,128)} %param.9) | copy-start | bytes 49156
where the time goes:
time: 208 us; the launch traced here: 207 us
  local copies, waits for them, and re-layouts  161 us (77%)
  blocking collectives  35.8 us (17%)
  other arithmetic  8.57 us (4%)
    gather x2, local copies, waits for them, and re-layouts, build_panel(): looked = jnp.take(coef_table, table_index, axis=0)  131 us
    all_gather x1, blocking collectives, on_device(): lax.all_gather(p_panel, 'row', axis=1, tiled=True)  23.7 us
    concatenate x1, local copies, waits for them, and re-layouts, stack_tables(): return jnp.transpose(jnp.concatenate([flat_eps, flat_inv], 1), (1, 0))  19.3 us
    all_to_all x1, blocking collectives, on_device(): lax.all_to_all(product_tile, 'row', split_axis=1, concat_axis=2, tiled=True)  12.1 us

commit v1 on v0

v1 whole, which is shorter than its diff:
```python
import functools

import jax
import jax.numpy as jnp
from jax import lax
from jax.experimental import pallas as pl
from jax.experimental.pallas import tpu as pltpu
from jax.sharding import PartitionSpec as P

LANES = 128
SUB = 8
UNROLL = 8


def round_up(value, step):
    return -(-value // step) * step


def build_q(me, extent, dims, eps_ref, inv_ref, wave_ref, harm_s, harm_v, panel_s, tab, part, q_ref):
    harm_total, cols, depth = dims
    half = (extent - 1) // 4
    window = round_up(2 * half + 1, SUB)
    rows_tab = round_up(extent + window - 2 * half - 1, SUB)
    i32 = jnp.int32
    lane = lax.broadcasted_iota(i32, (SUB, LANES), 1)
    sub = lax.broadcasted_iota(i32, (SUB, LANES), 0)
    first = pl.multiple_of(me * cols, cols)
    orders = harm_v[:, pl.ds(first, cols)]
    m_col = jnp.broadcast_to(orders[0:1, :], (SUB, cols))
    n_col = jnp.broadcast_to(orders[1:2, :], (SUB, cols))
    row_pick = half - m_col - sub
    col_base = 2 * half - n_col
    own = jnp.where(sub == 0, first + lane, -1)

    def block(step, carry):
        for u in range(UNROLL):
            k = step * UNROLL + u
            row = panel_s[k]
            bottom = row >= harm_total
            h = jnp.where(bottom, row - harm_total, row)
            m = harm_s[0, h]
            n = harm_s[1, h]
            start = n + half
            base = jnp.where(bottom, 4 * rows_tab, 0) + m + half
            index = (n + col_base) & (LANES - 1)
            low = lane >= start
            values = []
            for c in range(2):
                acc = jnp.zeros((SUB, LANES), jnp.float32)
                for i in range(window // SUB):
                    at = base + (2 * c * rows_tab + i * SUB)
                    left = tab[pl.ds(at, SUB), :]
                    right = tab[pl.ds(at + rows_tab, SUB), :]
                    both = jnp.where(low, left, right)
                    got = jnp.take_along_axis(both, index, axis=1, mode="promise_in_bounds")
                    acc = jnp.where(row_pick == i * SUB, got, acc)
                values.append(acc)
            wave_x = wave_ref[0] + m.astype(jnp.float32) * wave_ref[2]
            wave_y = wave_ref[1] + n.astype(jnp.float32) * wave_ref[3]
            sign0 = jnp.where(bottom, -1.0, 0.0)
            sign1 = jnp.where(bottom, 0.0, 1.0)
            diag0 = jnp.where(bottom, wave_y * wave_y, wave_x * wave_y)
            diag1 = jnp.where(bottom, -wave_x * wave_y, -wave_x * wave_x)
            on = own == h
            here = pl.ds(u * SUB, SUB)
            part[0, here, :] = values[0] * sign0 + jnp.where(on, diag0, 0.0)
            part[1, here, :] = values[0] * sign1 + jnp.where(on, diag1, 0.0)
            part[2, here, :] = values[1] * sign0
            part[3, here, :] = values[1] * sign1
        rows = pl.ds(pl.multiple_of(step * UNROLL, UNROLL), UNROLL)
        for c in range(4):
            total = part[c, pl.ds(0, UNROLL, stride=SUB), :]
            for s in range(1, SUB):
                total = total + part[c, pl.ds(s, UNROLL, stride=SUB), :]
            q_ref[rows, c * LANES : (c + 1) * LANES] = total
        return carry

    lax.fori_loop(0, depth // UNROLL, block, 0)


def fill_tables(extent, rows_tab, eps_ref, inv_ref, tab):
    for t, ref in enumerate((inv_ref, eps_ref)):
        for c in range(2):
            at = (4 * t + 2 * c) * rows_tab
            tab[at : at + extent, :] = ref[c, :, 0:LANES]
            tab[at + rows_tab : at + rows_tab + extent, 0 : extent - LANES] = ref[c, :, LANES:extent]


def kernel(
    n, extent, dims, p_ref, eps_ref, inv_ref, wave_ref, harm_s, harm_v, panel_s, target_ref, out_ref,
    tab, part, q_ref, p_all, prod, send_p, recv_p, send_o, recv_o, own_sem,
):
    harm_total, cols, depth = dims
    me = lax.axis_index("row")
    half = (extent - 1) // 4
    window = round_up(2 * half + 1, SUB)
    rows_tab = round_up(extent + window - 2 * half - 1, SUB)
    here = p_ref.shape[1]
    rows = n * here
    wide = 2 * cols

    barrier = pltpu.get_barrier_semaphore()

    def peer(d):
        return lax.rem(me + d, n)

    def greet(d, carry):
        pl.semaphore_signal(barrier, inc=1, device_id={"row": peer(d)}, device_id_type=pl.DeviceIdType.MESH)
        return carry

    lax.fori_loop(1, n, greet, 0)
    fill_tables(extent, rows_tab, eps_ref, inv_ref, tab)
    pl.semaphore_wait(barrier, n - 1)

    def p_copy(d):
        return pltpu.make_async_remote_copy(
            src_ref=p_ref,
            dst_ref=p_all.at[me],
            send_sem=send_p.at[d],
            recv_sem=recv_p.at[d],
            device_id={"row": peer(d)},
            device_id_type=pl.DeviceIdType.MESH,
        )

    def start_p(d, carry):
        p_copy(d).start()
        return carry

    lax.fori_loop(1, n, start_p, 0)
    p_all[me] = p_ref[...]

    build_q(me, extent, dims, eps_ref, inv_ref, wave_ref, harm_s, harm_v, panel_s, tab, part, q_ref)

    def wait_p(d, carry):
        p_copy(d).wait()
        return carry

    lax.fori_loop(1, n, wait_p, 0)

    pick = (lax.broadcasted_iota(jnp.int32, (rows, rows), 0) == target_ref[...]).astype(jnp.float32)
    q = q_ref[...]

    def permuted(c):
        return lax.dot_general(
            pick, p_all[:, c].reshape(rows, depth), (((0,), (0,)), ((), ())),
            precision=lax.Precision.HIGHEST, preferred_element_type=jnp.float32,
        )

    def times(left):
        return jnp.dot(left, q, precision=lax.Precision.HIGHEST, preferred_element_type=jnp.float32)

    by_real = times(permuted(0))
    by_imag = times(permuted(1))
    prod[:, 0] = (by_real[:, :wide] - by_imag[:, wide:]).reshape(n, here, wide)
    prod[:, 1] = (by_real[:, wide:] + by_imag[:, :wide]).reshape(n, here, wide)

    mine = pl.ds(pl.multiple_of(me * wide, wide), wide)

    def o_copy(d):
        return pltpu.make_async_remote_copy(
            src_ref=prod.at[peer(d)],
            dst_ref=out_ref.at[:, :, mine],
            send_sem=send_o.at[d],
            recv_sem=recv_o.at[d],
            device_id={"row": peer(d)},
            device_id_type=pl.DeviceIdType.MESH,
        )

    def start_o(d, carry):
        o_copy(d).start()
        return carry

    lax.fori_loop(1, n, start_o, 0)
    keep = pltpu.make_async_copy(prod.at[me], out_ref.at[:, :, mine], own_sem)
    keep.start()
    keep.wait()

    def wait_o(d, carry):
        o_copy(d).wait()
        return carry

    lax.fori_loop(1, n, wait_o, 0)


def on_device(n, p_panel, eps_coef, inv_coef, wave, harmonics, panel, row_target):
    extent = eps_coef.shape[1]
    harm_total = harmonics.shape[1]
    cols = harm_total // n
    depth = panel.shape[0]
    here = p_panel.shape[1]
    half = (extent - 1) // 4
    window = round_up(2 * half + 1, SUB)
    rows_tab = round_up(extent + window - 2 * half - 1, SUB)
    vmem = pl.BlockSpec(memory_space=pltpu.VMEM)
    smem = pl.BlockSpec(memory_space=pltpu.SMEM)
    f32 = jnp.float32
    return pl.pallas_call(
        functools.partial(kernel, n, extent, (harm_total, cols, depth)),
        out_shape=jax.ShapeDtypeStruct((2, here, n * 2 * cols), f32),
        in_specs=[vmem, vmem, vmem, smem, smem, vmem, smem, vmem],
        out_specs=vmem,
        scratch_shapes=[
            pltpu.VMEM((8 * rows_tab, LANES), f32),
            pltpu.VMEM((4, UNROLL * SUB, LANES), f32),
            pltpu.VMEM((depth, 4 * cols), f32),
            pltpu.VMEM((n, 2, here, depth), f32),
            pltpu.VMEM((n, 2, here, 2 * cols), f32),
            pltpu.SemaphoreType.DMA((n,)),
            pltpu.SemaphoreType.DMA((n,)),
            pltpu.SemaphoreType.DMA((n,)),
            pltpu.SemaphoreType.DMA((n,)),
            pltpu.SemaphoreType.DMA,
        ],
        compiler_params=pltpu.CompilerParams(
            collective_id=0, has_side_effects=True, vmem_limit_bytes=40 * 1024 * 1024
        ),
    )(p_panel, eps_coef, inv_coef, wave, harmonics, harmonics, panel, row_target.reshape(1, -1))


def solution(mesh):
    in_specs = (
        P(None, ("freq", "row"), None),
        P("freq", None, None),
        P("freq", None, None),
        P("freq"),
        P(),
        P(),
        P(),
    )
    return jax.shard_map(
        functools.partial(on_device, mesh.shape["row"]),
        mesh=mesh,
        in_specs=in_specs,
        out_specs=P(None, ("freq", "row"), None),
        check_vma=False,
    )
```

time: 208 us -> 27.6 us (0.13)
  local copies, waits for them, and re-layouts: 161 us -> 2.54 us
  blocking collectives: 35.8 us -> 0 us
  Pallas kernels: 0 us -> 24.6 us
  other arithmetic: 8.57 us -> 0 us
    gather x5 -> x0, local copies, waits for them, and re-layouts: 136 us -> none  [the longest x2 131 us: build_panel(): looked = jnp.take(coef_table, table_index, axis=0)]
    pallas_call x0 -> x1, Pallas kernels: none -> 24.6 us  [on_device(): pl.pallas_call(functools.partial(kernel, n, extent, (harm_total, cols, de...]
    all_gather x1 -> x0, blocking collectives: 23.7 us -> none  [on_device(): lax.all_gather(p_panel, 'row', axis=1, tiled=True)]
    concatenate x1 -> x0, local copies, waits for them, and re-layouts: 19.3 us -> none  [stack_tables(): return jnp.transpose(jnp.concatenate([flat_eps, flat_inv], 1), (1, 0))]
    all_to_all x1 -> x0, blocking collectives: 12.1 us -> none  [on_device(): lax.all_to_all(product_tile, 'row', split_axis=1, concat_axis=2, tiled=True)]
    mul x2 -> x0, other arithmetic: 5.18 us -> none  [the longest x1 2.59 us: build_panel(): wave_x * wave_y * on_diag]
    slice x2 -> x0, local copies, waits for them, and re-layouts: 2.27 us -> none  [the longest x1 1.46 us: build_panel(): wave_y = (wave[1] + n_row.astype(jnp.float32) * wave[3])[:, None]]
where the time goes in v1:
time: 27.6 us; the launch traced here: 27.2 us
  Pallas kernels  24.6 us (89%)
  local copies, waits for them, and re-layouts  2.54 us (9%)
    pallas_call x1, Pallas kernels, on_device(): pl.pallas_call(functools.partial(kernel, n, extent, (harm_total, cols, de...  24.6 us
    unnamed x15, local copies, waits for them, and re-layouts  2.54 us

profile of v1, /device:TPU:1, one launch (start us, length us, event | category | flops | bytes accessed | tf_op | source)
XLA Modules:
  0.0 27.2 jit_solution(6261809425629769811)
XLA Ops:
  0.0 0.0 copy-start.5
  0.0 1.1 %copy.8.eps_ref = f32[2,201,201]{2,1,0:T(8,128)S(1)} copy(f32[2,201,201]{2,0,1:T(2,128)} %param.8) | data formatting | bytes 646416 | tf_op args[1]
  1.1 0.0 copy-done.5
  1.1 0.0 copy-start
  1.1 0.0 copy-start.1
  1.1 0.0 copy-start.2
  1.1 0.0 copy-start.3
  1.1 0.0 copy-start.4
  1.2 0.6 %copy-done = s32[2,2048]{1,0:T(2,128)S(1)} copy-done((s32[2,2048]{1,0:T(2,128)S(1)}, s32[2,2048]{1,0:T(2,128)}, u32[]{:S(2)}) %copy-start) | copy-done | bytes 16408
  1.8 0.0 copy-done.1
  1.9 0.0 copy-done.2
  1.9 0.0 copy-done.3
  1.9 0.0 copy-done.4
  1.9 24.6 %shard_map.73 = f32[2,8,4096]{2,1,0:T(8,128)S(1)} custom-call(f32[2,8,256]{2,1,0:T(8,128)S(1)} %copy-done.1, f32[2,201,201]{2,1,0:T(8,128)S(1)} %copy.8.eps_ref, f32[2,201,201]{2,1,0:T(8,128)S(1)} %copy.9.inv_ref, f32[4]{0:T(128)S(1)} %copy-done.3, s32[2,2048]{1,0:T(2,128)S(1)} %copy-done, s32[2,2048]{1,0:T(2,128)S(1)} %copy-done, s32[256]{0:T(256)S(1)} %copy-done.2, ...), custom_call_target="tpu_custom_call" | custom-call | tf_op jit(solution)/shard_map/pallas_call | solution.py:197
  26.5 0.7 %copy.11 = f32[2,8,4096]{2,1,0:T(8,128)} copy(f32[2,8,4096]{2,1,0:T(8,128)S(1)} %shard_map.73) | data formatting | bytes 524288
  (1 shorter events, 0.0 us)
Async XLA Ops:
  0.0 1.1 %copy-start.5 = (f32[2,201,201]{2,0,1:T(2,128)S(1)}, f32[2,201,201]{2,0,1:T(2,128)}, u32[]{:S(2)}) copy-start(f32[2,201,201]{2,0,1:T(2,128)} %param.9) | copy-start | bytes 969628
  1.1 0.7 %copy-start = (s32[2,2048]{1,0:T(2,128)S(1)}, s32[2,2048]{1,0:T(2,128)}, u32[]{:S(2)}) copy-start(s32[2,2048]{1,0:T(2,128)} %harm_v.1) | copy-start | bytes 49156
  1.1 0.7 %copy-start.1 = (f32[2,8,256]{2,1,0:T(8,128)S(1)}, f32[2,8,256]{2,1,0:T(8,128)}, u32[]{:S(2)}) copy-start(f32[2,8,256]{2,1,0:T(8,128)} %p_ref.1) | copy-start | bytes 49156
  1.1 0.7 %copy-start.2 = (s32[256]{0:T(256)S(1)}, s32[256]{0:T(256)}, u32[]{:S(2)}) copy-start(s32[256]{0:T(256)} %panel_s.1) | copy-start | bytes 3076
  1.1 0.7 %copy-start.3 = (f32[4]{0:T(128)S(1)}, f32[4]{0:T(128)}, u32[]{:S(2)}) copy-start(f32[4]{0:T(128)} %wave_ref.1) | copy-start | bytes 52
  1.1 0.7 %copy-start.4 = (s32[128]{0:T(128)S(1)}, s32[128]{0:T(128)}, u32[]{:S(2)}) copy-start(s32[128]{0:T(128)} %param.13) | copy-start | bytes 1540

commit v2 on v1

--- a/solution.py
+++ b/solution.py
@@ -9,15 +9,15 @@
 
 LANES = 128
 SUB = 8
-UNROLL = 8
+UNROLL = 16
 
 
 def round_up(value, step):
     return -(-value // step) * step
 
 
-def build_q(me, extent, dims, eps_ref, inv_ref, wave_ref, harm_s, harm_v, panel_s, tab, part, q_ref):
-    harm_total, cols, depth = dims
+def build_q(me, extent, dims, span, wave_ref, harm_s, harm_v, panel_s, tab, part, q_ref):
+    harm_total, cols, _ = dims
     half = (extent - 1) // 4
     window = round_up(2 * half + 1, SUB)
     rows_tab = round_up(extent + window - 2 * half - 1, SUB)
@@ -75,7 +75,7 @@
             q_ref[rows, c * LANES : (c + 1) * LANES] = total
         return carry
 
-    lax.fori_loop(0, depth // UNROLL, block, 0)
+    lax.fori_loop(span[0], span[1], block, 0)
 
 
 def fill_tables(extent, rows_tab, eps_ref, inv_ref, tab):
@@ -109,7 +109,15 @@
         return carry
 
     lax.fori_loop(1, n, greet, 0)
+    p_all[me] = p_ref[...]
     fill_tables(extent, rows_tab, eps_ref, inv_ref, tab)
+
+    def build(begin, end):
+        build_q(me, extent, dims, (begin, end), wave_ref, harm_s, harm_v, panel_s, tab, part, q_ref)
+
+    steps = depth // UNROLL
+    early = steps // 4
+    build(0, early)
     pl.semaphore_wait(barrier, n - 1)
 
     def p_copy(d):
@@ -127,9 +135,7 @@
         return carry
 
     lax.fori_loop(1, n, start_p, 0)
-    p_all[me] = p_ref[...]
-
-    build_q(me, extent, dims, eps_ref, inv_ref, wave_ref, harm_s, harm_v, panel_s, tab, part, q_ref)
+    build(early, steps)
 
     def wait_p(d, carry):
         p_copy(d).wait()

time: 27.6 us -> 25.1 us (0.909)
  Pallas kernels: 24.6 us -> 22.3 us
    pallas_call x1, Pallas kernels: 24.6 us -> 22.3 us  [on_device(): pl.pallas_call(functools.partial(kernel, n, extent, (harm_total, cols, de...]
where the time goes in v2:
time: 25.1 us; the launch traced here: 24.9 us
  Pallas kernels  22.3 us (89%)
  local copies, waits for them, and re-layouts  2.54 us (10%)
    pallas_call x1, Pallas kernels, on_device(): pl.pallas_call(functools.partial(kernel, n, extent, (harm_total, cols, de...  22.3 us
    unnamed x15, local copies, waits for them, and re-layouts  2.54 us

profile of v2, /device:TPU:1, one launch (start us, length us, event | category | flops | bytes accessed | tf_op | source)
XLA Modules:
  0.0 24.9 jit_solution(2300879270811749001)
XLA Ops:
  0.0 0.0 copy-start.5
  0.0 1.1 %copy.8.eps_ref = f32[2,201,201]{2,1,0:T(8,128)S(1)} copy(f32[2,201,201]{2,0,1:T(2,128)} %param.8) | data formatting | bytes 646416 | tf_op args[1]
  1.1 0.0 copy-done.5
  1.1 0.0 copy-start
  1.1 0.0 copy-start.1
  1.1 0.0 copy-start.2
  1.1 0.0 copy-start.3
  1.1 0.0 copy-start.4
  1.2 0.6 %copy-done = s32[2,2048]{1,0:T(2,128)S(1)} copy-done((s32[2,2048]{1,0:T(2,128)S(1)}, s32[2,2048]{1,0:T(2,128)}, u32[]{:S(2)}) %copy-start) | copy-done | bytes 16408
  1.8 0.0 copy-done.1
  1.9 0.0 copy-done.2
  1.9 0.0 copy-done.3
  1.9 0.0 copy-done.4
  1.9 22.3 %shard_map.73 = f32[2,8,4096]{2,1,0:T(8,128)S(1)} custom-call(f32[2,8,256]{2,1,0:T(8,128)S(1)} %copy-done.1, f32[2,201,201]{2,1,0:T(8,128)S(1)} %copy.8.eps_ref, f32[2,201,201]{2,1,0:T(8,128)S(1)} %copy.9.inv_ref, f32[4]{0:T(128)S(1)} %copy-done.3, s32[2,2048]{1,0:T(2,128)S(1)} %copy-done, s32[2,2048]{1,0:T(2,128)S(1)} %copy-done, s32[256]{0:T(256)S(1)} %copy-done.2, ...), custom_call_target="tpu_custom_call" | custom-call | tf_op jit(solution)/shard_map/pallas_call | solution.py:203
  24.2 0.7 %copy.11 = f32[2,8,4096]{2,1,0:T(8,128)} copy(f32[2,8,4096]{2,1,0:T(8,128)S(1)} %shard_map.73) | data formatting | bytes 524288
  (1 shorter events, 0.0 us)
Async XLA Ops:
  0.0 1.1 %copy-start.5 = (f32[2,201,201]{2,0,1:T(2,128)S(1)}, f32[2,201,201]{2,0,1:T(2,128)}, u32[]{:S(2)}) copy-start(f32[2,201,201]{2,0,1:T(2,128)} %param.9) | copy-start | bytes 969628
  1.1 0.7 %copy-start = (s32[2,2048]{1,0:T(2,128)S(1)}, s32[2,2048]{1,0:T(2,128)}, u32[]{:S(2)}) copy-start(s32[2,2048]{1,0:T(2,128)} %harm_v.1) | copy-start | bytes 49156
  1.1 0.7 %copy-start.1 = (f32[2,8,256]{2,1,0:T(8,128)S(1)}, f32[2,8,256]{2,1,0:T(8,128)}, u32[]{:S(2)}) copy-start(f32[2,8,256]{2,1,0:T(8,128)} %p_ref.1) | copy-start | bytes 49156
  1.1 0.7 %copy-start.2 = (s32[256]{0:T(256)S(1)}, s32[256]{0:T(256)}, u32[]{:S(2)}) copy-start(s32[256]{0:T(256)} %panel_s.1) | copy-start | bytes 3076
  1.1 0.7 %copy-start.3 = (f32[4]{0:T(128)S(1)}, f32[4]{0:T(128)}, u32[]{:S(2)}) copy-start(f32[4]{0:T(128)} %wave_ref.1) | copy-start | bytes 52
  1.1 0.7 %copy-start.4 = (s32[128]{0:T(128)S(1)}, s32[128]{0:T(128)}, u32[]{:S(2)}) copy-start(s32[128]{0:T(128)} %param.13) | copy-start | bytes 1540
